TPU v7x, 32 devices: a whole 2x2x4 slice. The times are simulated.
32 devices in a mesh: groups: 2 (over y), seq: 4 (over z), head: 4 (over x, core).
Axes of the slice: x: 2, y: 2, z: 4, core: 2. Of those that a mesh axis runs over, the one named last changes fastest.
Arguments:
- raw_tokens: bfloat16 [4096, 4096], P(('groups', 'seq', 'head')), parts along dimension 0, may hold values from -6 to 6
- x_branch: bfloat16 [4096, 4096], P(('groups', 'seq'), 'head'), parts along dimension 0, may hold values from -6 to 6
- merge_list: int32 [4096, 2], P(('groups', 'seq')), parts along dimension 0, may hold values from 0 to 127
- lengths: int32 [32], P(('groups', 'seq')), parts along dimension 0, may hold values from 48 to 128, as said below
- log_decay: float32 [64, 4096], P('head', ('groups', 'seq')), parts along dimension 1, may hold values from -1.3 to 0
- init_state: float32 [128, 64, 128], P(('groups', 'head')), parts along dimension 0, may hold values from -12 to 12
- state_proj: bfloat16 [4096, 256], P(None, 'head'), may hold values from -0.005859375 to 0.005859375
- rate_proj: bfloat16 [4096, 64], P(None, 'head'), may hold values from -0.1875 to 0.1875
- step_bias: float32 [64], P('head'), may hold values from -2 to 1
- skip_gain: float32 [64], P('head'), may hold values from 0.1 to 1.9
- out_proj: bfloat16 [4096, 4096], P('head'), may hold values from -0.09375 to 0.09375
Outputs:
- out: bfloat16 [4096, 4096], P(('groups', 'seq', 'head')), parts along dimension 0
There are 2 independent parts, one for each index of `groups`. A program takes and returns all parts, laid end to end along the dimension named above; an argument that names none is the same for every part. Nothing has to cross between parts.
Inputs may be any that keep to these rules, and one draw needn't show every extreme that they name: `merge_list`: each entry is a row position inside its own row's aligned block of 128 token rows. `lengths`: the number of used rows at the start of an aligned block of 128 token rows; the other rows of the block are padding.
All inputs are finite; a program needn't handle non-finite values.
Results may differ from a plain program's by a relative error of at most 0.014.
Values may be sent and summed in bfloat16 or wider, within the bound.
A program may use at most 128 MiB of HBM per device.

v0:
```python
import jax
import jax.numpy as jnp
from jax import lax
from jax.sharding import PartitionSpec as P

STATE = 128
BLOCK = 256
MERGE = 128


def merge_rows(row_block, merge_list):
    row_count = row_block.shape[0]
    block_start = jnp.arange(row_count, dtype=jnp.int32) // MERGE * MERGE
    first_rows = jnp.take(row_block, block_start + merge_list[:, 0], axis=0).astype(jnp.float32)
    second = jnp.take(row_block, block_start + merge_list[:, 1], axis=0).astype(jnp.float32)
    return ((first_rows + second) * 0.5).astype(jnp.bfloat16)


def on_device(
    raw_tokens,
    x_branch,
    merge_list,
    lengths,
    log_decay,
    init_state,
    state_proj,
    rate_proj,
    step_bias,
    skip_gain,
    out_proj,
):
    own_rows = raw_tokens.shape[0]
    row_total = x_branch.shape[0]
    head_count = log_decay.shape[0]
    inner_width = x_branch.shape[1]
    head_width = inner_width // head_count
    block_count = row_total // BLOCK
    own_list = lax.dynamic_slice_in_dim(merge_list, lax.axis_index("head") * own_rows, own_rows, 0)
    merged_own = merge_rows(raw_tokens, own_list)
    slot_ids = jnp.arange(MERGE, dtype=jnp.int32)
    used_mask = (slot_ids[None, :] < lengths[:, None]).reshape(row_total).astype(jnp.float32)
    own_columns = state_proj.shape[1]
    joined = jnp.concatenate([state_proj, rate_proj], axis=1)
    projected = jnp.dot(
        lax.all_gather(merged_own, "head", axis=0, tiled=True),
        joined,
        preferred_element_type=jnp.float32,
    )
    state_part = projected[:, :own_columns].astype(jnp.bfloat16)
    state_maps = lax.all_gather(state_part, "head", axis=1, tiled=True)
    rate_pre = projected[:, own_columns:]
    step_size = jax.nn.softplus(rate_pre + step_bias[None, :]) * used_mask[:, None]
    log_rate = log_decay * used_mask[None, :]
    merged_x = merge_rows(x_branch, merge_list).reshape(block_count, BLOCK, head_count, head_width)
    b_blocks = state_maps[:, :STATE].reshape(block_count, BLOCK, STATE)
    c_blocks = state_maps[:, STATE:].reshape(block_count, BLOCK, STATE)
    step_blocks = step_size.reshape(block_count, BLOCK, head_count).transpose(2, 0, 1)
    rate_blocks = log_rate.reshape(head_count, block_count, BLOCK)
    position = jnp.arange(BLOCK, dtype=jnp.int32)
    causal = position[:, None] >= position[None, :]
    upper_ones = causal.T.astype(jnp.float32)
    cumulative = jnp.einsum("hck,ki->hci", rate_blocks, upper_ones, precision=lax.Precision.HIGHEST)
    scores = jnp.einsum("cin,cjn->cij", c_blocks, b_blocks, preferred_element_type=jnp.float32)
    spread = jnp.where(
        causal[None, None], cumulative[:, :, :, None] - cumulative[:, :, None, :], 0.0
    )
    decays = jnp.where(causal[None, None], jnp.exp(spread), 0.0)
    weight = (scores[None] * decays * step_blocks[:, :, None, :]).astype(jnp.bfloat16)
    inside = jnp.einsum("hcij,cjhp->cihp", weight, merged_x, preferred_element_type=jnp.float32)
    last_log = cumulative[:, :, -1]
    scaled = (jnp.exp(last_log[:, :, None] - cumulative) * step_blocks).transpose(1, 2, 0)[
        :, :, :, None
    ] * merged_x.astype(jnp.float32)
    scaled = scaled.astype(jnp.bfloat16)
    fresh_state = jnp.einsum("cjhp,cjn->chpn", scaled, b_blocks, preferred_element_type=jnp.float32)

    def advance(carry_state, inputs_now):
        decay_now, fresh_now = inputs_now
        return (decay_now[:, None, None] * carry_state + fresh_now, carry_state)

    local_end, local_enter = lax.scan(
        advance, jnp.zeros_like(init_state), (jnp.exp(last_log).T, fresh_state)
    )
    total_log = jnp.sum(last_log, axis=1)
    decay_logs = lax.all_gather(total_log[None, :], "seq", axis=0, tiled=True)
    my_rank = lax.axis_index("seq")
    device_rank = jnp.arange(decay_logs.shape[0], dtype=jnp.int32)
    log_in = jnp.sum(jnp.where(device_rank[:, None] < my_rank, decay_logs, 0.0), axis=0)
    running_logs = jnp.cumsum(decay_logs, axis=0)
    shard_part = lax.all_gather(
        local_end[None].astype(jnp.bfloat16), "seq", axis=0, tiled=True
    ).astype(jnp.float32)
    part_rows = shard_part.shape[0]
    source_rank = jnp.arange(part_rows, dtype=jnp.int32)
    earlier_rows = source_rank[:, None] < my_rank
    factor = jnp.where(
        earlier_rows, jnp.exp(jnp.where(earlier_rows, log_in[None, :] - running_logs, 0.0)), 0.0
    )
    inc_state = jnp.zeros_like(init_state) + jnp.sum(factor[:, :, None, None] * shard_part, axis=0)
    inc_decay = jnp.exp(log_in)
    incoming = inc_decay[:, None, None] * init_state + inc_state
    enter_decay = jnp.exp(jnp.cumsum(last_log, axis=1) - last_log)
    entering = local_enter + enter_decay.T[:, :, None, None] * incoming[None]
    carried = entering.astype(jnp.bfloat16)
    across = (
        jnp.einsum("cin,chpn->cihp", c_blocks, carried, preferred_element_type=jnp.float32)
        * jnp.exp(cumulative).transpose(1, 2, 0)[:, :, :, None]
    )
    skipped = skip_gain[None, None, :, None] * merged_x.astype(jnp.float32)
    mixed = (
        (inside + across + skipped).reshape(row_total, inner_width) * used_mask[:, None]
    ).astype(jnp.bfloat16)
    return lax.psum_scatter(
        jnp.dot(mixed, out_proj, preferred_element_type=jnp.float32).astype(jnp.bfloat16),
        "head",
        scatter_dimension=0,
        tiled=True,
    )


def solution(mesh):
    return jax.shard_map(
        on_device,
        mesh=mesh,
        in_specs=(
            P(("groups", "seq", "head"), None),
            P(("groups", "seq"), "head"),
            P(("groups", "seq"), None),
            P(("groups", "seq")),
            P("head", ("groups", "seq")),
            P(("groups", "head"), None, None),
            P(None, "head"),
            P(None, "head"),
            P("head"),
            P("head"),
            P("head", None),
        ),
        out_specs=P(("groups", "seq", "head"), None),
        check_vma=False,
    )
```

profile of v0, /device:TPU:29, one launch (start us, length us, event | category | flops | bytes accessed | tf_op | source)
XLA Modules:
  0.0 159.0 jit_solution(14893664499410678456)
XLA Ops:
  6.5 0.8 constant_dynamic-slice_fusion.1
  7.3 0.4 copy-done
  7.8 2.2 %gather_fusion.3 = bf16[128,4096]{1,0:T(8,128)(2,1)} fusion(bf16[128,4096]{1,0:T(8,128)(2,1)S(1)} %copy-done, s32[1024]{0:T(1024)S(1)} %get-tuple-element.83), kind=kCustom, calls=%fused_computation.3.clone | custom fusion | bytes 2097664 | tf_op jit(solution)/shard_map/jit(_take)/gather | solution.py:15
  9.9 2.2 %gather_fusion.2 = bf16[128,4096]{1,0:T(8,128)(2,1)} fusion(bf16[128,4096]{1,0:T(8,128)(2,1)S(1)} %copy-done, s32[1024]{0:T(1024)S(1)} %get-tuple-element.84), kind=kCustom, calls=%fused_computation.1.clone | custom fusion | bytes 2097664 | tf_op jit(solution)/shard_map/jit(_take)/gather | solution.py:14
  12.2 3.2 %multiply_convert_fusion.3 = bf16[128,4096]{1,0:T(8,128)(2,1)} fusion(bf16[128,4096]{1,0:T(8,128)(2,1)} %gather_fusion.3, bf16[128,4096]{1,0:T(8,128)(2,1)} %gather_fusion.2, pred[128]{0:T(512)(128)(4,1)S(1)} %get-tuple-element.79, pred[128]{0:T(512)(128)(4,1)S(1)} %get-tuple-element.67), kind=kLoop, calls=%fused_computation.25 | loop fusion | flops 3670016 | bytes 3145984 | tf_op jit(solution)/shard_map/convert_element_type | solution.py:16
  15.5 2.8 %gather_fusion = bf16[512,1024]{1,0:T(8,128)(2,1)} fusion(bf16[512,1024]{1,0:T(8,128)(2,1)S(1)} %copy-done.1, s32[1024]{0:T(1024)S(1)} %pad_clamp_fusion.3), kind=kCustom, calls=%fused_computation.clone | custom fusion | bytes 2099200 | tf_op jit(solution)/shard_map/jit(_take)/gather | solution.py:14
  18.3 2.8 %gather_fusion.1 = bf16[512,1024]{1,0:T(8,128)(2,1)} fusion(bf16[512,1024]{1,0:T(8,128)(2,1)S(1)} %copy-done.1, s32[1024]{0:T(1024)S(1)} %pad_clamp_fusion.2), kind=kCustom, calls=%fused_computation.2.clone | custom fusion | bytes 2099200 | tf_op jit(solution)/shard_map/jit(_take)/gather | solution.py:15
  21.1 2.1 %multiply_convert_fusion.4 = bf16[512,1024]{1,0:T(8,128)(2,1)S(1)} fusion(bf16[512,1024]{1,0:T(8,128)(2,1)} %gather_fusion.1, bf16[512,1024]{1,0:T(8,128)(2,1)} %gather_fusion, pred[512]{0:T(512)(128)(4,1)S(1)} %get-tuple-element.81, pred[512]{0:T(512)(128)(4,1)S(1)} %get-tuple-element.82), kind=kLoop, calls=%fused_computation.26 | loop fusion | flops 3670016 | bytes 3146752 | tf_op jit(solution)/shard_map/convert_element_type | solution.py:16
  23.2 2.3 %reshape.199 = bf16[2,256,16,64]{3,2,1,0:T(8,128)(2,1)} reshape(bf16[512,1024]{1,0:T(8,128)(2,1)S(1)} %multiply_convert_fusion.4) | data formatting | bytes 2097152 | tf_op jit(solution)/shard_map/reshape | solution.py:54
  25.6 4.0 %copy.31 = bf16[2,256,16,64]{1,3,2,0:T(8,128)(2,1)} copy(bf16[2,256,16,64]{3,2,1,0:T(8,128)(2,1)} %reshape.199) | data formatting | bytes 2097152 | tf_op jit(solution)/shard_map/reshape | solution.py:54
  29.6 0.3 fusion.22
  30.1 21.3 %all-gather.5.cloned.1.call-done = bf16[512,4096]{1,0:T(8,128)(2,1)} async-done(((bf16[128,4096]{1,0:T(8,128)(2,1)}), bf16[512,4096]{1,0:T(8,128)(2,1)}) %all-gather.5.cloned.1.call-update) | async-done | bytes 4194320 | tf_op jit(solution)/shard_map/all_gather | solution.py:45
  51.4 3.6 %fusion.15 = f32[512,80]{0,1:T(8,128)S(1)} fusion(bf16[512,4096]{1,0:T(8,128)(2,1)} %all-gather.5.cloned.1.call-done, bf16[4096,16]{0,1:T(8,128)(2,1)S(1)} %copy-done.9, bf16[4096,64]{0,1:T(8,128)(2,1)S(1)} %copy-done.8), kind=kOutput, calls=%fused_computation.31 | convolution fusion | flops 336855040 | bytes 5013504 | tf_op jit(solution)/shard_map/dot_general | solution.py:44
  55.1 5.9 %all_gather.13 = bf16[512,256]{0,1:T(8,128)(2,1)S(1)} all-gather(bf16[512,64]{0,1:T(8,128)(2,1)S(1)} %slice.58), channel_id=1, replica_groups=mesh['groups'=2,'seq'=4,'head'=4] {'head'}, dimensions={1}, use_global_device_ids=true | all-gather | bytes 327680 | tf_op jit(solution)/shard_map/all_gather | solution.py:50
  61.1 1.7 %fusion.11 = f32[2,16,64,128]{3,2,1,0:T(8,128)S(1)} fusion(bf16[2,256,16,64]{1,3,2,0:T(8,128)(2,1)} %copy.31, f32[2,256,16]{1,2,0:T(8,128)S(1)} %get-tuple-element.74, bf16[2,256,128,1]{1,0,2,3:T(2,128)(2,1)S(1)} %bitcast.86), kind=kOutput, calls=%fused_computation.27 | convolution fusion | flops 135790592 | bytes 2260992 | tf_op jit(solution)/shard_map/cjhp,cjn->chpn/dot_general | solution.py:75
  62.8 2.0 %while.13 = (s32[]{:T(128)}, f32[16,64,128]{2,1,0:T(8,128)S(1)}, f32[2,16,64,128]{3,2,1,0:T(8,128)}, f32[2,16]{1,0:T(2,128)S(1)}, f32[2,16,64,128]{3,2,1,0:T(8,128)S(1)}, /*index=5*/s32[]{:T(128)}, s32[]{:T(128)}) while((s32[]{:T(128)}, f32[16,64,128]{2,1,0:T(8,128)S(1)}, f32[2,16,64,128]{3,2,1,0:T(8,128)}, f32[2,16]{1,0:T(2,128)S(1)}, ...), condition=%wide.region_1.4_spmd.clone, body=%wide.region_0.0_spmd.clone.sunk | while | flops 524291 | bytes 2621740 | solution.py:81
  62.9 0.9 bitcast_dynamic-update-slice_fusion.2
  63.9 0.8 bitcast_dynamic-update-slice_fusion.2
  64.8 0.8 convert_element_type.73
  65.7 0.6 dynamic-slice
  67.0 0.2 dynamic-update-slice
  67.2 6.5 %all-reduce = f32[64]{0:T(128)S(1)} all-reduce(f32[64]{0:T(128)S(1)} %dynamic-update-slice), channel_id=2, replica_groups=mesh['groups'=2,'seq'=4,'head'=4] {'seq'}, use_global_device_ids=true, to_apply=%add | all-reduce | flops 64 | bytes 512
  74.2 0.3 fusion.24
  74.4 17.6 %all-gather.7.cloned.1.call-done = bf16[64,64,128]{2,1,0:T(8,128)(2,1)} async-done(((bf16[16,64,128]{2,1,0:T(8,128)(2,1)}), bf16[64,64,128]{2,1,0:T(8,128)(2,1)}) %all-gather.7.cloned.1.call-update) | async-done | bytes 1048592 | tf_op jit(solution)/shard_map/all_gather | solution.py:90
  92.0 1.5 fusion.10
  93.6 1.2 multiply_add_fusion
  94.8 0.5 fusion.19
  95.2 0.7 copy-done.2
  95.9 2.8 %fusion.9 = f32[2,256,16,64]{1,3,2,0:T(8,128)S(1)} fusion(bf16[2,256,16,64]{1,3,2,0:T(8,128)(2,1)S(1)} %copy-done.2, f32[2,256,16,64]{1,3,2,0:T(8,128)S(1)} %fusion.19, f32[16,2,256]{2,0,1:T(8,128)S(1)} %copy.30, f32[16,2,256]{2,0,1:T(8,128)S(1)} %fusion.22, f32[2,256,256]{2,1,0:T(8,128)S(1)} %fusion.24, pred[256,256]{1,0:T(8,128)(4,1)S(1)} %iota_compare_fusion, ...), kind=kOutput, calls=%fused_computation.20 | convolution fusion | flops 283639808 | bytes 5931072 | tf_op jit(solution)/shard_map/hcij,cjhp->cihp/dot_general | solution.py:69
  98.8 1.6 %copy.36 = f32[2,256,16,64]{1,0,3,2:T(2,128)S(1)} copy(f32[2,256,16,64]{1,3,2,0:T(8,128)S(1)} %fusion.9) | data formatting | bytes 4194304 | tf_op jit(solution)/shard_map/add | solution.py:111
  100.6 6.4 %convolution_convert_fusion = bf16[512,4096]{1,0:T(8,128)(2,1)} fusion(bf16[1024,4096]{1,0:T(8,128)(2,1)S(1)} %bitcast.96, f32[512,1024]{0,1:T(8,128)S(1)} %bitcast.81, f32[512]{0:T(512)S(1)} %convert_bitcast_fusion), kind=kOutput, calls=%fused_computation.9 | convolution fusion | flops 4298113024 | bytes 14682112 | tf_op jit(solution)/shard_map/dot_general | solution.py:114
  107.1 45.4 %reduce-scatter.2.cloned.1.call-done = bf16[128,4096]{1,0:T(8,128)(2,1)} async-done(((bf16[512,4096]{1,0:T(8,128)(2,1)}), bf16[128,4096]{1,0:T(8,128)(2,1)}) %reduce-scatter.2.cloned.1.call-update) | async-done | bytes 1048592 | tf_op jit(solution)/shard_map/reduce_scatter | solution.py:113
  (69 shorter events, 1.6 us)
Async XLA Ops:
  6.5 1.2 copy-start
  6.5 44.9 %all-gather.5.cloned.1.call-start = ((), (), s32[]{:S(2)}) async-start(), calls=%async_computation.1 | async-start | bytes 5242880 | tf_op jit(solution)/shard_map/all_gather | solution.py:45
  12.2 3.3 %copy-start.5 = (s32[512,2]{0,1:T(2,128)S(1)}, s32[512,2]{0,1:T(2,128)}, u32[]{:S(2)}) copy-start(s32[512,2]{0,1:T(2,128)} %param.19) | copy-start | bytes 12292
  12.2 3.4 %copy-start.1 = (bf16[512,1024]{1,0:T(8,128)(2,1)S(1)}, bf16[512,1024]{1,0:T(8,128)(2,1)}, u32[]{:S(2)}) copy-start(bf16[512,1024]{1,0:T(8,128)(2,1)} %param.18) | copy-start | bytes 3145732
  15.4 76.6 %all-gather.7.cloned.1.call-start = ((), (), s32[]{:S(2)}) async-start(), calls=%async_computation.3 | async-start | bytes 1310720 | tf_op jit(solution)/shard_map/all_gather | solution.py:90
  25.5 4.0 %copy-start.7 = (s32[4]{0:T(128)S(1)}, s32[4]{0:T(128)}, u32[]{:S(2)}) copy-start(s32[4]{0:T(128)} %param.20) | copy-start | bytes 52
  25.5 4.0 %copy-start.4 = (f32[16,512]{1,0:T(8,128)S(1)}, f32[16,512]{1,0:T(8,128)}, u32[]{:S(2)}) copy-start(f32[16,512]{1,0:T(8,128)} %param.21) | copy-start | bytes 98308
  25.5 25.9 %copy-start.8 = (bf16[4096,64]{0,1:T(8,128)(2,1)S(1)}, bf16[4096,64]{0,1:T(8,128)(2,1)}, u32[]{:S(2)}) copy-start(bf16[4096,64]{0,1:T(8,128)(2,1)} %param.23) | copy-start | bytes 1572868
  25.5 25.9 %copy-start.9 = (bf16[4096,16]{0,1:T(8,128)(2,1)S(1)}, bf16[4096,16]{0,1:T(8,128)(2,1)}, u32[]{:S(2)}) copy-start(bf16[4096,16]{0,1:T(8,128)(2,1)} %param.24) | copy-start | bytes 393220
  30.1 24.9 %copy-start.6 = (f32[16]{0:T(128)S(1)}, f32[16]{0:T(128)}, u32[]{:S(2)}) copy-start(f32[16]{0:T(128)} %param.25) | copy-start | bytes 196
  62.8 2.9 %copy-start.11 = (u32[32]{0:T(128)S(1)}, u32[32]{0:T(128)}, u32[]{:S(2)}) copy-start(u32[32]{0:T(128)} %constant.91) | copy-start | bytes 388
  65.6 86.9 %reduce-scatter.2.cloned.1.call-start = ((), (), s32[]{:S(2)}) async-start(), calls=%async_computation.2 | async-start | bytes 5242880 | tf_op jit(solution)/shard_map/reduce_scatter | solution.py:113
  74.1 20.6 %copy-start.3 = (f32[2,16,64,128]{3,2,1,0:T(8,128)S(1)}, f32[2,16,64,128]{3,2,1,0:T(8,128)}, u32[]{:S(2)}) copy-start(f32[2,16,64,128]{3,2,1,0:T(8,128)} %get-tuple-element.35) | copy-start | bytes 3145732
  94.7 1.2 copy-start.2
  94.7 1.2 copy-start.10
  94.7 5.9 %slice-start = ((s8[8388608]{0:T(1024)(128)(4,1)}), s8[4194304]{0:T(1024)(128)(4,1)S(1)}, s32[]{:S(2)}) async-start(s8[8388608]{0:T(1024)(128)(4,1)} %bitcast.95), calls=%async_computation.4 | async-start | bytes 8388608
  95.9 4.7 %slice-start.1 = ((s8[8388608]{0:T(1024)(128)(4,1)}), s8[4194304]{0:T(1024)(128)(4,1)S(1)}, s32[]{:S(2)}) async-start(s8[8388608]{0:T(1024)(128)(4,1)} %bitcast.95), calls=%async_computation.5 | async-start | bytes 8388608
Sparse Core Ops, SparseCore 0:
  15.5 35.8 all-gather.4
  65.7 26.2 all-gather.6
  107.2 45.2 reduce-scatter.1
where the time goes:
time: 161 us; the launch traced here: 159 us
  waiting for transfers between devices  84.3 us (52%)
  local copies, waits for them, and re-layouts  21.1 us (13%)
  matrix products  15.5 us (10%)
  between operations  14.1 us (9%)
  blocking collectives  12.4 us (8%)
  other arithmetic  11.5 us (7%)
    reduce_scatter x1, waiting for transfers between devices, on_device(): lax.psum_scatter(jnp.dot(mixed, out_proj, preferred_element_type=jnp.floa...  45.4 us
    all_gather x1, waiting for transfers between devices, on_device(): lax.all_gather(merged_own, 'head', axis=0, tiled=True)  21.3 us
    all_gather x1, waiting for transfers between devices, on_device(): lax.all_gather(local_end[None].astype(jnp.bfloat16), 'seq', axis=0, tiled...  17.6 us
    unnamed x1, blocking collectives  6.54 us
    dot_general x1, matrix products, on_device(): jnp.dot(mixed, out_proj, preferred_element_type=jnp.float32)  6.41 us
    reshape x2, local copies, waits for them, and re-layouts, on_device(): merge_rows(x_branch, merge_list)  6.3 us
    all_gather x1, blocking collectives, on_device(): state_maps = lax.all_gather(state_part, 'head', axis=1, tiled=True)  5.89 us
    convert_element_type x2, other arithmetic, merge_rows(): return ((first_rows + second) * 0.5).astype(jnp.bfloat16)  5.3 us
  transfers between devices with their start and end apart: 3, of which 3 were waited for; matrix products, arithmetic and copies ran while one was open for 10% of the time, Pallas kernels for 0%

commit v1 on v0

v1 whole, which is shorter than its diff:
```python
import functools

import jax
import jax.numpy as jnp
from jax import lax
from jax.experimental import pallas as pl
from jax.experimental.pallas import tpu as pltpu
from jax.sharding import PartitionSpec as P

STATE = 128
BLOCK = 256
MERGE = 128
LANES = 128
WEIGHT_PIECES = 4
STATE_PIECES = 4
OUT_PIECES = 8
MESH = pl.DeviceIdType.MESH
F32 = jnp.float32
BF16 = jnp.bfloat16
HIGH = lax.Precision.HIGHEST


def dot(a, b, precision=None):
    return jnp.dot(a, b, preferred_element_type=F32, precision=precision)


def dot_t(a, b, precision=None):
    return lax.dot_general(
        a, b, (((1,), (1,)), ((), ())), preferred_element_type=F32, precision=precision
    )


def kernel(
    seq_count,
    lengths,
    step_bias,
    skip_gain,
    merge_list,
    log_decay,
    init_state,
    raw_hbm,
    x_hbm,
    state_hbm,
    rate_hbm,
    proj_hbm,
    out_ref,
    raw,
    x_rows,
    proj,
    state_w,
    rate_w,
    pick,
    merged,
    merged_x,
    decay,
    enter_exp,
    last_factor,
    steps,
    maps,
    rate_send,
    rate_got,
    fresh,
    state_in,
    state_out,
    carried,
    inside,
    mixed,
    mine,
    pair_send,
    pair_got,
    cross_send,
    cross_got,
    load_sem,
    w_send,
    w_recv,
    m_send,
    m_recv,
    s_send,
    s_recv,
    p_send,
    p_recv,
    c_send,
    c_recv,
):
    head = lax.axis_index("head")
    rank = lax.axis_index("seq")
    core = lax.rem(head, 2)
    sib = head + 1 - 2 * core
    cross = lax.rem(head + 2, 4)
    diag = 3 - head
    heads = log_decay.shape[0]
    width = merged_x.shape[2]
    pairs = heads // 2
    model = raw.shape[1]
    piece = model // WEIGHT_PIECES

    loads = [
        pltpu.make_async_copy(raw_hbm, raw, load_sem.at[0]),
        pltpu.make_async_copy(x_hbm, x_rows, load_sem.at[1]),
        pltpu.make_async_copy(state_hbm, state_w.at[head], load_sem.at[2]),
        pltpu.make_async_copy(rate_hbm, rate_w.at[head], load_sem.at[3]),
        pltpu.make_async_copy(proj_hbm, proj, load_sem.at[4]),
    ]
    for load in loads:
        load.start()

    barrier = pltpu.get_barrier_semaphore()
    for peer in (sib, cross, diag):
        pl.semaphore_signal(barrier, inc=1, device_id={"head": peer}, device_id_type=MESH)
    for peer in (lax.rem(rank + 1, seq_count), lax.rem(rank + seq_count - 1, seq_count)):
        pl.semaphore_signal(barrier, inc=1, device_id={"seq": peer}, device_id_type=MESH)
    pl.semaphore_wait(barrier, 5)

    def weight_copies(kind, p, peer, owner, forward):
        span = pl.ds(p * piece, piece)
        out = []
        for which, (source, held) in enumerate(((state_hbm, state_w), (rate_hbm, rate_w))):
            out.append(
                pltpu.make_async_remote_copy(
                    src_ref=held.at[owner, :, span] if forward else source.at[:, span],
                    dst_ref=held.at[owner, :, span],
                    send_sem=w_send.at[kind, p, which],
                    recv_sem=w_recv.at[kind, p, which],
                    device_id={"head": peer},
                    device_id_type=MESH,
                )
            )
        return out

    to_cross = [weight_copies(0, p, cross, head, False) for p in range(WEIGHT_PIECES)]
    to_sib = [weight_copies(1, p, sib, head, False) for p in range(WEIGHT_PIECES)]
    passed = [weight_copies(2, p, sib, cross, True) for p in range(WEIGHT_PIECES)]
    for group in (to_cross, to_sib):
        for copies in group:
            for copy in copies:
                copy.start()

    row_id = lax.broadcasted_iota(jnp.int32, (MERGE, MERGE), 0)
    for b in range(4):
        chosen = merge_list[:, b * MERGE : (b + 1) * MERGE]
        first = jnp.where(row_id == chosen[0:1], 0.5, 0.0)
        second = jnp.where(row_id == chosen[1:2], 0.5, 0.0)
        pick[b] = jnp.transpose(first + second).astype(BF16)
    loads[0].wait()
    own_pick = pick[head]
    for p in range(WEIGHT_PIECES):
        cols = slice(p * piece, (p + 1) * piece)
        merged[:, cols] = dot(own_pick, raw[:, cols]).astype(BF16)
    loads[1].wait()
    for b in range(4):
        rows = slice(b * MERGE, (b + 1) * MERGE)
        to = slice((b % 2) * MERGE, (b % 2 + 1) * MERGE)
        merged_x[b // 2, to, :] = dot(pick[b], x_rows[rows, :]).astype(BF16)

    first_half = lax.broadcasted_iota(jnp.int32, (BLOCK, LANES), 1) < LANES // 2
    top_half = lax.broadcasted_iota(jnp.int32, (STATE, LANES), 1) < LANES // 2
    row_i = lax.broadcasted_iota(jnp.int32, (BLOCK, BLOCK), 0)
    col_i = lax.broadcasted_iota(jnp.int32, (BLOCK, BLOCK), 1)
    causal = row_i >= col_i
    lower = jnp.where(causal, 1.0, 0.0)
    upper = jnp.where(row_i <= col_i, 1.0, 0.0)
    lane_i = lax.broadcasted_iota(jnp.int32, (heads, BLOCK), 1)

    def used_lanes(k):
        limit = jnp.where(lane_i < MERGE, lengths[2 * k], lengths[2 * k + 1] + MERGE)
        return jnp.where(lane_i < limit, 1.0, 0.0)

    def pass_on(p):
        for copy in to_cross[p]:
            copy.wait_recv()
        for copy in passed[p]:
            copy.start()

    done = 0
    for k in range(2):
        rates = log_decay[:, k * BLOCK : (k + 1) * BLOCK] * used_lanes(k)
        along = dot(rates, upper, HIGH)
        down = dot_t(lower, rates, HIGH)
        last_factor[k] = jnp.exp(along[:, BLOCK - 1 : BLOCK] - along)
        grown = jnp.exp(down)
        for i in range(pairs):
            enter_exp[k, :, i * LANES : (i + 1) * LANES] = jnp.where(
                first_half, grown[:, 2 * i : 2 * i + 1], grown[:, 2 * i + 1 : 2 * i + 2]
            )
        for h in range(heads):
            spread = down[:, h : h + 1] - along[h : h + 1, :]
            decay[k, h] = jnp.exp(jnp.minimum(spread, 0.0)).astype(BF16)
            done += 1
            if done % (2 * heads // WEIGHT_PIECES) == 0:
                pass_on(done // (2 * heads // WEIGHT_PIECES) - 1)

    loads[2].wait()
    loads[3].wait()
    map_sum, rate_sum = None, None
    for p in range(WEIGHT_PIECES):
        for copy in to_sib[p] + passed[p]:
            copy.wait_recv()
        cols = slice(p * piece, (p + 1) * piece)
        tokens = merged[:, cols]
        map_part = dot_t(tokens, state_w[:, :, cols].reshape(2 * STATE, piece))
        rate_part = dot_t(rate_w[:, :, cols].reshape(4 * heads, piece), tokens)
        map_sum = map_part if p == 0 else map_sum + map_part
        rate_sum = rate_part if p == 0 else rate_sum + rate_part
    maps[head] = map_sum.astype(BF16)
    rate_send[...] = rate_sum.reshape(4, heads, MERGE)
    shared = []
    for which, peer in enumerate((cross, diag, sib)):
        for kind, (source, to) in enumerate(
            ((rate_send.at[peer], rate_got.at[head]), (maps.at[head], maps.at[head]))
        ):
            copy = pltpu.make_async_remote_copy(
                src_ref=source,
                dst_ref=to,
                send_sem=m_send.at[which, kind],
                recv_sem=m_recv.at[which, kind],
                device_id={"head": peer},
                device_id_type=MESH,
            )
            copy.start()
            shared.append(copy)
    rate_got[head] = rate_send[head]
    for copy in shared:
        copy.wait_recv()

    head_i = lax.broadcasted_iota(jnp.int32, (heads, BLOCK), 0)
    bias = jnp.zeros((heads, BLOCK), F32)
    for h in range(heads):
        bias = jnp.where(head_i == h, step_bias[h], bias)
    for k in range(2):
        value = jnp.concatenate([rate_got[2 * k], rate_got[2 * k + 1]], axis=1) + bias
        size = jnp.maximum(value, 0.0) + jnp.log1p(jnp.exp(-jnp.abs(value)))
        size = size * used_lanes(k)
        steps[k] = size
        factor = last_factor[k] * size
        b_part = maps[2 * k : 2 * k + 2, :, :STATE].reshape(BLOCK, STATE)
        b_turned = jnp.transpose(b_part.astype(F32))
        for i in range(pairs):
            cols = slice(i * LANES, (i + 1) * LANES)
            x_pair = merged_x[k, :, cols]
            one = dot((b_turned * factor[2 * i : 2 * i + 1]).astype(BF16), x_pair)
            two = dot((b_turned * factor[2 * i + 1 : 2 * i + 2]).astype(BF16), x_pair)
            fresh[k, :, cols] = jnp.where(top_half, one, two)

    state_width = width // STATE_PIECES
    onward = [
        pltpu.make_async_remote_copy(
            src_ref=state_out.at[q],
            dst_ref=state_in.at[q],
            send_sem=s_send.at[q],
            recv_sem=s_recv.at[q],
            device_id={"seq": lax.rem(rank + 1, seq_count)},
            device_id_type=MESH,
        )
        for q in range(STATE_PIECES)
    ]

    def advance(q):
        cols = slice(q * state_width, (q + 1) * state_width)
        entering = state_in[q]
        middle = (
            enter_exp[0, BLOCK - 1 : BLOCK, cols] * entering.astype(F32) + fresh[0, :, cols]
        )
        carried[0, :, cols] = entering
        carried[1, :, cols] = middle.astype(BF16)
        leaving = enter_exp[1, BLOCK - 1 : BLOCK, cols] * middle + fresh[1, :, cols]
        state_out[q] = leaving.astype(BF16)

        @pl.when(rank < seq_count - 1)
        def _():
            onward[q].start()

    def inside_of(k):
        both = maps[pl.ds(2 * k, 2)].reshape(BLOCK, 2 * STATE)
        scores = dot_t(both[:, STATE:], both[:, :STATE])
        scores = jnp.where(causal, scores, 0.0).astype(BF16)
        sizes = steps[k].astype(BF16)
        for i in range(pairs):
            cols = slice(i * LANES, (i + 1) * LANES)
            x_pair = merged_x[k, :, cols]
            one = dot(scores * (decay[k, 2 * i] * sizes[2 * i : 2 * i + 1]), x_pair)
            two = dot(scores * (decay[k, 2 * i + 1] * sizes[2 * i + 1 : 2 * i + 2]), x_pair)
            gains = jnp.where(first_half, skip_gain[2 * i], skip_gain[2 * i + 1])
            inside[:, cols] = jnp.where(first_half, one, two) + gains * x_pair.astype(F32)

    def mix(k):
        c_part = maps[pl.ds(2 * k, 2), :, STATE:].reshape(BLOCK, STATE)
        limit = jnp.where(row_i < MERGE, lengths[2 * k], lengths[2 * k + 1] + MERGE)
        used = row_i < limit
        for i in range(width // BLOCK):
            cols = slice(i * BLOCK, (i + 1) * BLOCK)
            across = dot(c_part, carried[k, :, cols]) * enter_exp[k, :, cols]
            value = jnp.where(used, inside[:, cols] + across, 0.0).astype(BF16)
            mixed[pl.ds(2 * k, 2), :, cols] = value.reshape(2, MERGE, BLOCK)

    far, near = cross // 2, head // 2

    @pl.when(rank == 0)
    def _():
        per = state_width // LANES
        for i in range(pairs):
            turned = jnp.transpose(init_state[2 * i : 2 * i + 2].reshape(LANES, STATE))
            at = slice((i % per) * LANES, (i % per + 1) * LANES)
            state_in[i // per, :, at] = turned.astype(BF16)
        for q in range(STATE_PIECES):
            advance(q)

    inside_of(far)

    @pl.when(rank > 0)
    def _():
        for q in range(STATE_PIECES):
            onward[q].wait_recv()
            advance(q)

    mix(far)

    out_width = model // OUT_PIECES
    loads[4].wait()

    def swap(turn, n):
        return pltpu.make_async_remote_copy(
            src_ref=pair_send.at[turn, n],
            dst_ref=pair_got.at[turn, n],
            send_sem=p_send.at[turn, n],
            recv_sem=p_recv.at[turn, n],
            device_id={"head": sib},
            device_id_type=MESH,
        )

    swaps = [[swap(turn, n) for n in range(OUT_PIECES)] for turn in range(2)]
    crossings = [
        pltpu.make_async_remote_copy(
            src_ref=cross_send.at[n],
            dst_ref=cross_got.at[n],
            send_sem=c_send.at[n],
            recv_sem=c_recv.at[n],
            device_id={"head": cross},
            device_id_type=MESH,
        )
        for n in range(OUT_PIECES)
    ]

    def send_across(n):
        swaps[0][n].wait_recv()
        cross_send[n] = (mine[n] + pair_got[0, n].astype(F32)).astype(BF16)
        crossings[n].start()

    rows = jnp.concatenate([mixed[diag], mixed[cross]], axis=0)
    for n in range(OUT_PIECES):
        cols = slice(n * out_width, (n + 1) * out_width)
        terms = dot(rows, proj[:, cols])
        pair_send[0, n] = terms[:MERGE].astype(BF16)
        swaps[0][n].start()
        mine[n] = terms[MERGE:]
        if n > 0:
            send_across(n - 1)
    send_across(OUT_PIECES - 1)

    inside_of(near)
    mix(near)
    rows = jnp.concatenate([mixed[sib], mixed[head]], axis=0)
    for n in range(OUT_PIECES):
        cols = slice(n * out_width, (n + 1) * out_width)
        terms = dot(rows, proj[:, cols])
        pair_send[1, n] = terms[:MERGE].astype(BF16)
        swaps[1][n].start()
        mine[n] = terms[MERGE:]
    for n in range(OUT_PIECES):
        cols = slice(n * out_width, (n + 1) * out_width)
        swaps[1][n].wait_recv()
        total = mine[n] + pair_got[1, n].astype(F32)
        crossings[n].wait_recv()
        out_ref[:, cols] = (total + cross_got[n].astype(F32)).astype(BF16)

    for group in to_cross + to_sib + passed:
        for copy in group:
            copy.wait_send()
    for copy in shared + swaps[0] + swaps[1] + crossings:
        copy.wait_send()

    @pl.when(rank < seq_count - 1)
    def _():
        for copy in onward:
            copy.wait_send()


def on_device(
    seq_count,
    raw_tokens,
    x_branch,
    merge_list,
    lengths,
    log_decay,
    init_state,
    state_proj,
    rate_proj,
    step_bias,
    skip_gain,
    out_proj,
):
    own_rows, model = raw_tokens.shape
    width = x_branch.shape[1]
    heads = log_decay.shape[0]
    out_width = model // OUT_PIECES
    blocks = x_branch.shape[0] // BLOCK
    state_width = width // STATE_PIECES
    smem = pl.BlockSpec(memory_space=pltpu.SMEM)
    vmem = pl.BlockSpec(memory_space=pltpu.VMEM)
    hbm = pl.BlockSpec(memory_space=pl.ANY)
    dma = pltpu.SemaphoreType.DMA
    return pl.pallas_call(
        functools.partial(kernel, seq_count),
        out_shape=jax.ShapeDtypeStruct((own_rows, model), BF16),
        in_specs=[smem] * 3 + [vmem] * 3 + [hbm] * 5,
        out_specs=vmem,
        scratch_shapes=[
            pltpu.VMEM(raw_tokens.shape, BF16),
            pltpu.VMEM(x_branch.shape, BF16),
            pltpu.VMEM(out_proj.shape, BF16),
            pltpu.VMEM((4, state_proj.shape[1], model), BF16),
            pltpu.VMEM((4, heads, model), BF16),
            pltpu.VMEM((4, MERGE, MERGE), BF16),
            pltpu.VMEM((own_rows, model), BF16),
            pltpu.VMEM((blocks, BLOCK, width), BF16),
            pltpu.VMEM((blocks, heads, BLOCK, BLOCK), BF16),
            pltpu.VMEM((blocks, BLOCK, width), F32),
            pltpu.VMEM((blocks, heads, BLOCK), F32),
            pltpu.VMEM((blocks, heads, BLOCK), F32),
            pltpu.VMEM((4, MERGE, 2 * STATE), BF16),
            pltpu.VMEM((4, heads, MERGE), F32),
            pltpu.VMEM((4, heads, MERGE), F32),
            pltpu.VMEM((blocks, STATE, width), F32),
            pltpu.VMEM((STATE_PIECES, STATE, state_width), BF16),
            pltpu.VMEM((STATE_PIECES, STATE, state_width), BF16),
            pltpu.VMEM((blocks, STATE, width), BF16),
            pltpu.VMEM((BLOCK, width), F32),
            pltpu.VMEM((4, MERGE, width), BF16),
            pltpu.VMEM((OUT_PIECES, MERGE, out_width), F32),
            pltpu.VMEM((2, OUT_PIECES, MERGE, out_width), BF16),
            pltpu.VMEM((2, OUT_PIECES, MERGE, out_width), BF16),
            pltpu.VMEM((OUT_PIECES, MERGE, out_width), BF16),
            pltpu.VMEM((OUT_PIECES, MERGE, out_width), BF16),
            dma((5,)),
            dma((3, WEIGHT_PIECES, 2)),
            dma((3, WEIGHT_PIECES, 2)),
            dma((3, 2)),
            dma((3, 2)),
            dma((STATE_PIECES,)),
            dma((STATE_PIECES,)),
            dma((2, OUT_PIECES)),
            dma((2, OUT_PIECES)),
            dma((OUT_PIECES,)),
            dma((OUT_PIECES,)),
        ],
        compiler_params=pltpu.CompilerParams(
            collective_id=0, has_side_effects=True, vmem_limit_bytes=56 * 1024 * 1024
        ),
    )(
        lengths,
        step_bias,
        skip_gain,
        merge_list.T,
        log_decay,
        init_state,
        raw_tokens,
        x_branch,
        state_proj.T,
        rate_proj.T,
        out_proj,
    )


def solution(mesh):
    return jax.shard_map(
        functools.partial(on_device, mesh.shape["seq"]),
        mesh=mesh,
        in_specs=(
            P(("groups", "seq", "head"), None),
            P(("groups", "seq"), "head"),
            P(("groups", "seq"), None),
            P(("groups", "seq")),
            P("head", ("groups", "seq")),
            P(("groups", "head"), None, None),
            P(None, "head"),
            P(None, "head"),
            P("head"),
            P("head"),
            P("head", None),
        ),
        out_specs=P(("groups", "seq", "head"), None),
        check_vma=False,
    )
```

time: 161 us -> 73.2 us (0.45); the launches traced: 159 us -> 73 us
  waiting for transfers between devices: 84.3 us -> 0 us
  Pallas kernels: 0 us -> 70.7 us
  local copies, waits for them, and re-layouts: 21.1 us -> 2.29 us
  matrix products: 15.5 us -> 0 us
  between operations: 14.1 us -> 0.01 us
  blocking collectives: 12.4 us -> 0 us
  other arithmetic: 11.5 us -> 0 us
    pallas_call x0 -> x1, Pallas kernels: none -> 70.7 us  [on_device(): pl.pallas_call(functools.partial(kernel, seq_count), out_shape=jax.ShapeD...]
    reduce_scatter x1 -> x0, waiting for transfers between devices: 45.4 us -> none  [on_device(): lax.psum_scatter(jnp.dot(mixed, out_proj, preferred_element_type=jnp.floa...]
    all_gather x2 -> x0, waiting for transfers between devices: 38.8 us -> none  [the longest x1 21.3 us: on_device(): lax.all_gather(merged_own, 'head', axis=0, tiled=True)]
    dot_general x7 -> x0, matrix products: 15.5 us -> none  [the longest x1 6.41 us: on_device(): jnp.dot(mixed, out_proj, preferred_element_type=jnp.float32)]
    gather x4 -> x0, local copies, waits for them, and re-layouts: 9.92 us -> none  [the longest x2 4.99 us: merge_rows(): jnp.take(row_block, block_start + merge_list[:, 0], axis=0)]
    unnamed x1 -> x0, blocking collectives: 6.54 us -> none
    reshape x5 -> x0, local copies, waits for them, and re-layouts: 6.4 us -> none  [the longest x2 6.3 us: on_device(): merge_rows(x_branch, merge_list)]
    convert_element_type x4 -> x0, other arithmetic: 6.12 us -> none  [the longest x2 5.3 us: merge_rows(): return ((first_rows + second) * 0.5).astype(jnp.bfloat16)]
  transfers between devices with their start and end apart: 3 -> 0, of which waited for: 3 -> 0; matrix products, arithmetic and copies ran while one was open for 10% -> 0% of each run, Pallas kernels for 0% -> 0%
where the time goes in v1:
time: 73.2 us; the launch traced here: 73 us
  Pallas kernels  70.7 us (97%)
  local copies, waits for them, and re-layouts  2.29 us (3%)
    pallas_call x1, Pallas kernels, on_device(): pl.pallas_call(functools.partial(kernel, seq_count), out_shape=jax.ShapeD...  70.7 us
    unnamed x1, local copies, waits for them, and re-layouts  2.29 us

profile of v1, /device:TPU:29, one launch (start us, length us, event | category | flops | bytes accessed | tf_op | source)
XLA Modules:
  0.0 73.0 jit_solution(15639800595913977418)
XLA Ops:
  0.0 70.7 %shard_map.109 = bf16[128,4096]{1,0:T(8,128)(2,1)} custom-call(s32[4]{0:T(128)} %lengths.1, f32[16]{0:T(128)} %step_bias.1, f32[16]{0:T(128)} %skip_gain.1, s32[2,512]{1,0:T(2,128)} %bitcast.5, f32[16,512]{1,0:T(8,128)} %log_decay.1, f32[16,64,128]{2,1,0:T(8,128)} %init_state.1, bf16[128,4096]{1,0:T(8,128)(2,1)} %raw_hbm.1, bf16[512,1024]{1,0:T(8,128)(2,1)} %x_hbm.1, ...), custom_call_target="tpu_custom_call" | custom-call | tf_op jit(solution)/shard_map/pallas_call | solution.py:411
  70.8 2.3 %copy.13 = bf16[128,4096]{1,0:T(8,128)(2,1)} copy(bf16[128,4096]{1,0:T(8,128)(2,1)} %shard_map.109) | data formatting | bytes 2097152

commit v2 on v1

--- a/solution.py
+++ b/solution.py
@@ -12,7 +12,7 @@
 MERGE = 128
 LANES = 128
 WEIGHT_PIECES = 4
-STATE_PIECES = 4
+STATE_PIECES = 8
 OUT_PIECES = 8
 MESH = pl.DeviceIdType.MESH
 F32 = jnp.float32
@@ -43,7 +43,8 @@
     state_hbm,
     rate_hbm,
     proj_hbm,
-    out_ref,
+    total_hbm,
+    cross_got,
     raw,
     x_rows,
     proj,
@@ -56,7 +57,8 @@
     enter_exp,
     last_factor,
     steps,
-    maps,
+    b_maps,
+    c_maps,
     rate_send,
     rate_got,
     fresh,
@@ -69,7 +71,7 @@
     pair_send,
     pair_got,
     cross_send,
-    cross_got,
+    total,
     load_sem,
     w_send,
     w_recv,
@@ -84,6 +86,7 @@
 ):
     head = lax.axis_index("head")
     rank = lax.axis_index("seq")
+    group = lax.axis_index("groups")
     core = lax.rem(head, 2)
     sib = head + 1 - 2 * core
     cross = lax.rem(head + 2, 4)
@@ -92,7 +95,7 @@
     width = merged_x.shape[2]
     pairs = heads // 2
     model = raw.shape[1]
-    piece = model // WEIGHT_PIECES
+    piece = model // (2 * WEIGHT_PIECES)
 
     loads = [
         pltpu.make_async_copy(raw_hbm, raw, load_sem.at[0]),
@@ -109,10 +112,13 @@
         pl.semaphore_signal(barrier, inc=1, device_id={"head": peer}, device_id_type=MESH)
     for peer in (lax.rem(rank + 1, seq_count), lax.rem(rank + seq_count - 1, seq_count)):
         pl.semaphore_signal(barrier, inc=1, device_id={"seq": peer}, device_id_type=MESH)
-    pl.semaphore_wait(barrier, 5)
-
-    def weight_copies(kind, p, peer, owner, forward):
-        span = pl.ds(p * piece, piece)
+    pl.semaphore_signal(barrier, inc=1, device_id={"groups": 1 - group}, device_id_type=MESH)
+    pl.semaphore_wait(barrier, 6)
+
+    def piece_at(half, p):
+        return pl.ds(pl.multiple_of((half * WEIGHT_PIECES + p) * piece, piece), piece)
+
+    def weight_copies(kind, p, peer, owner, span, forward):
         out = []
         for which, (source, held) in enumerate(((state_hbm, state_w), (rate_hbm, rate_w))):
             out.append(
@@ -121,19 +127,26 @@
                     dst_ref=held.at[owner, :, span],
                     send_sem=w_send.at[kind, p, which],
                     recv_sem=w_recv.at[kind, p, which],
-                    device_id={"head": peer},
+                    device_id=peer,
                     device_id_type=MESH,
                 )
             )
         return out
 
-    to_cross = [weight_copies(0, p, cross, head, False) for p in range(WEIGHT_PIECES)]
-    to_sib = [weight_copies(1, p, sib, head, False) for p in range(WEIGHT_PIECES)]
-    passed = [weight_copies(2, p, sib, cross, True) for p in range(WEIGHT_PIECES)]
-    for group in (to_cross, to_sib):
-        for copies in group:
-            for copy in copies:
-                copy.start()
+    order = range(WEIGHT_PIECES)
+    other = {"groups": 1 - group}
+    near_by = {"head": sib}
+    to_cross = [
+        weight_copies(0, p, {"head": cross}, head, piece_at(group, p), False) for p in order
+    ]
+    to_sib = weight_copies(1, 0, near_by, head, pl.ds(0, model), False)
+    to_group = [weight_copies(2, p, other, cross, piece_at(group, p), True) for p in order]
+    pass_first = [weight_copies(3, p, near_by, cross, piece_at(group, p), True) for p in order]
+    pass_second = [
+        weight_copies(4, p, near_by, cross, piece_at(1 - group, p), True) for p in order
+    ]
+    for copy in sum(to_cross, []) + to_sib:
+        copy.start()
 
     row_id = lax.broadcasted_iota(jnp.int32, (MERGE, MERGE), 0)
     for b in range(4):
@@ -143,7 +156,7 @@
         pick[b] = jnp.transpose(first + second).astype(BF16)
     loads[0].wait()
     own_pick = pick[head]
-    for p in range(WEIGHT_PIECES):
+    for p in range(2 * WEIGHT_PIECES):
         cols = slice(p * piece, (p + 1) * piece)
         merged[:, cols] = dot(own_pick, raw[:, cols]).astype(BF16)
     loads[1].wait()
@@ -165,11 +178,22 @@
         limit = jnp.where(lane_i < MERGE, lengths[2 * k], lengths[2 * k + 1] + MERGE)
         return jnp.where(lane_i < limit, 1.0, 0.0)
 
-    def pass_on(p):
+    def pass_x(p):
         for copy in to_cross[p]:
             copy.wait_recv()
-        for copy in passed[p]:
+        for copy in to_group[p] + pass_first[p]:
             copy.start()
+
+    def pass_y(p):
+        for copy in to_group[p]:
+            copy.wait_recv()
+        for copy in pass_second[p]:
+            copy.start()
+
+    passes = [functools.partial(pass_x, 0)]
+    for p in range(1, WEIGHT_PIECES):
+        passes += [functools.partial(pass_x, p), functools.partial(pass_y, p - 1)]
+    passes.append(functools.partial(pass_y, WEIGHT_PIECES - 1))
 
     done = 0
     for k in range(2):
@@ -186,60 +210,41 @@
             spread = down[:, h : h + 1] - along[h : h + 1, :]
             decay[k, h] = jnp.exp(jnp.minimum(spread, 0.0)).astype(BF16)
             done += 1
-            if done % (2 * heads // WEIGHT_PIECES) == 0:
-                pass_on(done // (2 * heads // WEIGHT_PIECES) - 1)
+            if done % (2 * heads // len(passes)) == 0:
+                passes[done // (2 * heads // len(passes)) - 1]()
 
     loads[2].wait()
     loads[3].wait()
     map_sum, rate_sum = None, None
-    for p in range(WEIGHT_PIECES):
-        for copy in to_sib[p] + passed[p]:
+    for copy in to_sib:
+        copy.wait_recv()
+    for p in range(2 * WEIGHT_PIECES):
+        part = p % WEIGHT_PIECES
+        for copy in (pass_first if p < WEIGHT_PIECES else pass_second)[part]:
             copy.wait_recv()
-        cols = slice(p * piece, (p + 1) * piece)
+        cols = piece_at(group if p < WEIGHT_PIECES else 1 - group, part)
         tokens = merged[:, cols]
         map_part = dot_t(tokens, state_w[:, :, cols].reshape(2 * STATE, piece))
         rate_part = dot_t(rate_w[:, :, cols].reshape(4 * heads, piece), tokens)
         map_sum = map_part if p == 0 else map_sum + map_part
         rate_sum = rate_part if p == 0 else rate_sum + rate_part
-    maps[head] = map_sum.astype(BF16)
+    b_maps[head] = map_sum[:, :STATE].astype(BF16)
+    c_maps[head] = map_sum[:, STATE:].astype(BF16)
     rate_send[...] = rate_sum.reshape(4, heads, MERGE)
-    shared = []
-    for which, peer in enumerate((cross, diag, sib)):
-        for kind, (source, to) in enumerate(
-            ((rate_send.at[peer], rate_got.at[head]), (maps.at[head], maps.at[head]))
-        ):
+    shared = [[], [], []]
+    for kind, to in enumerate((rate_got, b_maps, c_maps)):
+        for which, peer in enumerate((cross, diag, sib)):
             copy = pltpu.make_async_remote_copy(
-                src_ref=source,
-                dst_ref=to,
+                src_ref=rate_send.at[peer] if kind == 0 else to.at[head],
+                dst_ref=to.at[head],
                 send_sem=m_send.at[which, kind],
                 recv_sem=m_recv.at[which, kind],
                 device_id={"head": peer},
                 device_id_type=MESH,
             )
             copy.start()
-            shared.append(copy)
+            shared[kind].append(copy)
     rate_got[head] = rate_send[head]
-    for copy in shared:
-        copy.wait_recv()
-
-    head_i = lax.broadcasted_iota(jnp.int32, (heads, BLOCK), 0)
-    bias = jnp.zeros((heads, BLOCK), F32)
-    for h in range(heads):
-        bias = jnp.where(head_i == h, step_bias[h], bias)
-    for k in range(2):
-        value = jnp.concatenate([rate_got[2 * k], rate_got[2 * k + 1]], axis=1) + bias
-        size = jnp.maximum(value, 0.0) + jnp.log1p(jnp.exp(-jnp.abs(value)))
-        size = size * used_lanes(k)
-        steps[k] = size
-        factor = last_factor[k] * size
-        b_part = maps[2 * k : 2 * k + 2, :, :STATE].reshape(BLOCK, STATE)
-        b_turned = jnp.transpose(b_part.astype(F32))
-        for i in range(pairs):
-            cols = slice(i * LANES, (i + 1) * LANES)
-            x_pair = merged_x[k, :, cols]
-            one = dot((b_turned * factor[2 * i : 2 * i + 1]).astype(BF16), x_pair)
-            two = dot((b_turned * factor[2 * i + 1 : 2 * i + 2]).astype(BF16), x_pair)
-            fresh[k, :, cols] = jnp.where(top_half, one, two)
 
     state_width = width // STATE_PIECES
     onward = [
@@ -269,9 +274,45 @@
         def _():
             onward[q].start()
 
+    head_i = lax.broadcasted_iota(jnp.int32, (heads, BLOCK), 0)
+    bias = jnp.zeros((heads, BLOCK), F32)
+    for h in range(heads):
+        bias = jnp.where(head_i == h, step_bias[h], bias)
+    for copy in shared[0]:
+        copy.wait_recv()
+    factors = []
+    for k in range(2):
+        value = jnp.concatenate([rate_got[2 * k], rate_got[2 * k + 1]], axis=1) + bias
+        size = jnp.maximum(value, 0.0) + jnp.log1p(jnp.exp(-jnp.abs(value)))
+        size = size * used_lanes(k)
+        steps[k] = size
+        factors.append(last_factor[k] * size)
+    for copy in shared[1]:
+        copy.wait_recv()
+    turned_maps = [
+        jnp.transpose(b_maps[2 * k : 2 * k + 2].reshape(BLOCK, STATE).astype(F32))
+        for k in range(2)
+    ]
+    for i in range(pairs):
+        cols = slice(i * LANES, (i + 1) * LANES)
+        for k in range(2):
+            x_pair = merged_x[k, :, cols]
+            one, two = [
+                dot((turned_maps[k] * factors[k][h : h + 1]).astype(BF16), x_pair)
+                for h in (2 * i, 2 * i + 1)
+            ]
+            fresh[k, :, cols] = jnp.where(top_half, one, two)
+
+        @pl.when(rank == 0)
+        def _():
+            turned = jnp.transpose(init_state[2 * i : 2 * i + 2].reshape(LANES, STATE))
+            state_in[i] = turned.astype(BF16)
+            advance(i)
+
     def inside_of(k):
-        both = maps[pl.ds(2 * k, 2)].reshape(BLOCK, 2 * STATE)
-        scores = dot_t(both[:, STATE:], both[:, :STATE])
+        b_part = b_maps[pl.ds(2 * k, 2)].reshape(BLOCK, STATE)
+        c_part = c_maps[pl.ds(2 * k, 2)].reshape(BLOCK, STATE)
+        scores = dot_t(c_part, b_part)
         scores = jnp.where(causal, scores, 0.0).astype(BF16)
         sizes = steps[k].astype(BF16)
         for i in range(pairs):
@@ -283,7 +324,7 @@
             inside[:, cols] = jnp.where(first_half, one, two) + gains * x_pair.astype(F32)
 
     def mix(k):
-        c_part = maps[pl.ds(2 * k, 2), :, STATE:].reshape(BLOCK, STATE)
+        c_part = c_maps[pl.ds(2 * k, 2)].reshape(BLOCK, STATE)
         limit = jnp.where(row_i < MERGE, lengths[2 * k], lengths[2 * k + 1] + MERGE)
         used = row_i < limit
         for i in range(width // BLOCK):
@@ -294,19 +335,17 @@
 
     far, near = cross // 2, head // 2
 
-    @pl.when(rank == 0)
+    @pl.when(rank == 1)
     def _():
-        per = state_width // LANES
-        for i in range(pairs):
-            turned = jnp.transpose(init_state[2 * i : 2 * i + 2].reshape(LANES, STATE))
-            at = slice((i % per) * LANES, (i % per + 1) * LANES)
-            state_in[i // per, :, at] = turned.astype(BF16)
         for q in range(STATE_PIECES):
+            onward[q].wait_recv()
             advance(q)
 
+    for copy in shared[2]:
+        copy.wait_recv()
     inside_of(far)
 
-    @pl.when(rank > 0)
+    @pl.when(rank > 1)
     def _():
         for q in range(STATE_PIECES):
             onward[q].wait_recv()
@@ -331,7 +370,7 @@
     crossings = [
         pltpu.make_async_remote_copy(
             src_ref=cross_send.at[n],
-            dst_ref=cross_got.at[n],
+            dst_ref=cross_got.at[:, n * out_width : (n + 1) * out_width],
             send_sem=c_send.at[n],
             recv_sem=c_recv.at[n],
             device_id={"head": cross},
@@ -368,15 +407,16 @@
     for n in range(OUT_PIECES):
         cols = slice(n * out_width, (n + 1) * out_width)
         swaps[1][n].wait_recv()
-        total = mine[n] + pair_got[1, n].astype(F32)
-        crossings[n].wait_recv()
-        out_ref[:, cols] = (total + cross_got[n].astype(F32)).astype(BF16)
-
-    for group in to_cross + to_sib + passed:
-        for copy in group:
-            copy.wait_send()
-    for copy in shared + swaps[0] + swaps[1] + crossings:
+        total[:, cols] = (mine[n] + pair_got[1, n].astype(F32)).astype(BF16)
+    store = pltpu.make_async_copy(total, total_hbm, load_sem.at[5])
+    store.start()
+
+    groups = to_cross + [to_sib] + to_group + pass_first + pass_second + shared + swaps
+    for copy in sum(groups, []):
         copy.wait_send()
+    store.wait()
+    for copy in crossings:
+        copy.wait()
 
     @pl.when(rank < seq_count - 1)
     def _():
@@ -408,11 +448,11 @@
     vmem = pl.BlockSpec(memory_space=pltpu.VMEM)
     hbm = pl.BlockSpec(memory_space=pl.ANY)
     dma = pltpu.SemaphoreType.DMA
-    return pl.pallas_call(
+    total, arrived = pl.pallas_call(
         functools.partial(kernel, seq_count),
-        out_shape=jax.ShapeDtypeStruct((own_rows, model), BF16),
+        out_shape=[jax.ShapeDtypeStruct((own_rows, model), BF16)] * 2,
         in_specs=[smem] * 3 + [vmem] * 3 + [hbm] * 5,
-        out_specs=vmem,
+        out_specs=[hbm, hbm],
         scratch_shapes=[
             pltpu.VMEM(raw_tokens.shape, BF16),
             pltpu.VMEM(x_branch.shape, BF16),
@@ -426,7 +466,8 @@
             pltpu.VMEM((blocks, BLOCK, width), F32),
             pltpu.VMEM((blocks, heads, BLOCK), F32),
             pltpu.VMEM((blocks, heads, BLOCK), F32),
-            pltpu.VMEM((4, MERGE, 2 * STATE), BF16),
+            pltpu.VMEM((4, MERGE, STATE), BF16),
+            pltpu.VMEM((4, MERGE, STATE), BF16),
             pltpu.VMEM((4, heads, MERGE), F32),
             pltpu.VMEM((4, heads, MERGE), F32),
             pltpu.VMEM((blocks, STATE, width), F32),
@@ -439,12 +480,12 @@
             pltpu.VMEM((2, OUT_PIECES, MERGE, out_width), BF16),
             pltpu.VMEM((2, OUT_PIECES, MERGE, out_width), BF16),
             pltpu.VMEM((OUT_PIECES, MERGE, out_width), BF16),
-            pltpu.VMEM((OUT_PIECES, MERGE, out_width), BF16),
-            dma((5,)),
-            dma((3, WEIGHT_PIECES, 2)),
-            dma((3, WEIGHT_PIECES, 2)),
-            dma((3, 2)),
-            dma((3, 2)),
+            pltpu.VMEM((own_rows, model), BF16),
+            dma((6,)),
+            dma((5, WEIGHT_PIECES, 2)),
+            dma((5, WEIGHT_PIECES, 2)),
+            dma((3, 3)),
+            dma((3, 3)),
             dma((STATE_PIECES,)),
             dma((STATE_PIECES,)),
             dma((2, OUT_PIECES)),
@@ -468,6 +509,7 @@
         rate_proj.T,
         out_proj,
     )
+    return (total.astype(F32) + arrived.astype(F32)).astype(BF16)
 
 
 def solution(mesh):

time: 73.2 us -> 67.9 us (0.928)
  Pallas kernels: 70.7 us -> 64.9 us
  other arithmetic: 0 us -> 2.76 us
  local copies, waits for them, and re-layouts: 2.29 us -> 0 us
    pallas_call x1, Pallas kernels: 70.7 us -> 64.9 us  [on_device(): pl.pallas_call(functools.partial(kernel, seq_count), out_shape=[jax.Shape...]
    convert_element_type x0 -> x1, other arithmetic: none -> 2.76 us  [on_device(): return (total.astype(F32) + arrived.astype(F32)).astype(BF16)]
    unnamed x1 -> x0, local copies, waits for them, and re-layouts: 2.29 us -> none
where the time goes in v2:
time: 67.9 us; the launch traced here: 67.7 us
  Pallas kernels  64.9 us (96%)
  other arithmetic  2.76 us (4%)
    pallas_call x1, Pallas kernels, on_device(): pl.pallas_call(functools.partial(kernel, seq_count), out_shape=[jax.Shape...  64.9 us
    convert_element_type x1, other arithmetic, on_device(): return (total.astype(F32) + arrived.astype(F32)).astype(BF16)  2.76 us

profile of v2, /device:TPU:29, one launch (start us, length us, event | category | flops | bytes accessed | tf_op | source)
XLA Modules:
  0.0 67.7 jit_solution(16940609927176319785)
XLA Ops:
  0.0 64.9 %shard_map.109 = (bf16[128,4096]{1,0:T(8,128)(2,1)}, bf16[128,4096]{1,0:T(8,128)(2,1)}) custom-call(s32[4]{0:T(128)} %lengths.1, f32[16]{0:T(128)} %step_bias.1, f32[16]{0:T(128)} %skip_gain.1, s32[2,512]{1,0:T(2,128)} %bitcast.5, f32[16,512]{1,0:T(8,128)} %log_decay.1, f32[16,64,128]{2,1,0:T(8,128)} %init_state.1, bf16[128,4096]{1,0:T(8,128)(2,1)} %raw_hbm.1, ...), custom_call_target="tpu_custom_call" | custom-call | tf_op jit(solution)/shard_map/pallas_call | solution.py:451
  64.9 2.8 %add_convert_fusion = bf16[128,4096]{1,0:T(8,128)(2,1)} fusion(bf16[128,4096]{1,0:T(8,128)(2,1)} %get-tuple-element.8, bf16[128,4096]{1,0:T(8,128)(2,1)} %get-tuple-element.7), kind=kLoop, calls=%fused_computation | loop fusion | flops 2097152 | bytes 3145728 | tf_op jit(solution)/shard_map/convert_element_type | solution.py:512

commit v3 on v2

--- a/solution.py
+++ b/solution.py
@@ -37,7 +37,7 @@
     skip_gain,
     merge_list,
     log_decay,
-    init_state,
+    init_hbm,
     raw_hbm,
     x_hbm,
     state_hbm,
@@ -72,6 +72,7 @@
     pair_got,
     cross_send,
     total,
+    init_state,
     load_sem,
     w_send,
     w_recv,
@@ -97,22 +98,22 @@
     model = raw.shape[1]
     piece = model // (2 * WEIGHT_PIECES)
 
+    barrier = pltpu.get_barrier_semaphore()
+    for peer in (sib, cross, diag):
+        pl.semaphore_signal(barrier, inc=1, device_id={"head": peer}, device_id_type=MESH)
+    for peer in (lax.rem(rank + 1, seq_count), lax.rem(rank + seq_count - 1, seq_count)):
+        pl.semaphore_signal(barrier, inc=1, device_id={"seq": peer}, device_id_type=MESH)
+    pl.semaphore_signal(barrier, inc=1, device_id={"groups": 1 - group}, device_id_type=MESH)
     loads = [
         pltpu.make_async_copy(raw_hbm, raw, load_sem.at[0]),
         pltpu.make_async_copy(x_hbm, x_rows, load_sem.at[1]),
         pltpu.make_async_copy(state_hbm, state_w.at[head], load_sem.at[2]),
         pltpu.make_async_copy(rate_hbm, rate_w.at[head], load_sem.at[3]),
         pltpu.make_async_copy(proj_hbm, proj, load_sem.at[4]),
+        pltpu.make_async_copy(init_hbm, init_state, load_sem.at[6]),
     ]
-    for load in loads:
+    for load in loads[:4]:
         load.start()
-
-    barrier = pltpu.get_barrier_semaphore()
-    for peer in (sib, cross, diag):
-        pl.semaphore_signal(barrier, inc=1, device_id={"head": peer}, device_id_type=MESH)
-    for peer in (lax.rem(rank + 1, seq_count), lax.rem(rank + seq_count - 1, seq_count)):
-        pl.semaphore_signal(barrier, inc=1, device_id={"seq": peer}, device_id_type=MESH)
-    pl.semaphore_signal(barrier, inc=1, device_id={"groups": 1 - group}, device_id_type=MESH)
     pl.semaphore_wait(barrier, 6)
 
     def piece_at(half, p):
@@ -212,6 +213,9 @@
             done += 1
             if done % (2 * heads // len(passes)) == 0:
                 passes[done // (2 * heads // len(passes)) - 1]()
+
+    loads[4].start()
+    loads[5].start()
 
     loads[2].wait()
     loads[3].wait()
@@ -274,6 +278,8 @@
         def _():
             onward[q].start()
 
+    loads[5].wait()
+
     head_i = lax.broadcasted_iota(jnp.int32, (heads, BLOCK), 0)
     bias = jnp.zeros((heads, BLOCK), F32)
     for h in range(heads):
@@ -451,7 +457,7 @@
     total, arrived = pl.pallas_call(
         functools.partial(kernel, seq_count),
         out_shape=[jax.ShapeDtypeStruct((own_rows, model), BF16)] * 2,
-        in_specs=[smem] * 3 + [vmem] * 3 + [hbm] * 5,
+        in_specs=[smem] * 3 + [vmem] * 2 + [hbm] * 6,
         out_specs=[hbm, hbm],
         scratch_shapes=[
             pltpu.VMEM(raw_tokens.shape, BF16),
@@ -481,7 +487,8 @@
             pltpu.VMEM((2, OUT_PIECES, MERGE, out_width), BF16),
             pltpu.VMEM((OUT_PIECES, MERGE, out_width), BF16),
             pltpu.VMEM((own_rows, model), BF16),
-            dma((6,)),
+            pltpu.VMEM(init_state.shape, F32),
+            dma((7,)),
             dma((5, WEIGHT_PIECES, 2)),
             dma((5, WEIGHT_PIECES, 2)),
             dma((3, 3)),

time: 67.9 us -> 67.6 us (level)
  no operation moved by 1% of the time
where the time goes in v3:
time: 67.6 us; the launch traced here: 67.4 us
  Pallas kernels  64.6 us (96%)
  other arithmetic  2.76 us (4%)
    pallas_call x1, Pallas kernels, on_device(): pl.pallas_call(functools.partial(kernel, seq_count), out_shape=[jax.Shape...  64.6 us
    convert_element_type x1, other arithmetic, on_device(): return (total.astype(F32) + arrived.astype(F32)).astype(BF16)  2.76 us

profile of v3, /device:TPU:29, one launch (start us, length us, event | category | flops | bytes accessed | tf_op | source)
XLA Modules:
  0.0 67.4 jit_solution(5242147628727731194)
XLA Ops:
  0.0 64.6 %shard_map.109 = (bf16[128,4096]{1,0:T(8,128)(2,1)}, bf16[128,4096]{1,0:T(8,128)(2,1)}) custom-call(s32[4]{0:T(128)} %lengths.1, f32[16]{0:T(128)} %step_bias.1, f32[16]{0:T(128)} %skip_gain.1, s32[2,512]{1,0:T(2,128)} %bitcast.5, f32[16,512]{1,0:T(8,128)} %log_decay.1, f32[16,64,128]{2,1,0:T(8,128)} %init_hbm.1, bf16[128,4096]{1,0:T(8,128)(2,1)} %raw_hbm.1, ...), custom_call_target="tpu_custom_call" | custom-call | tf_op jit(solution)/shard_map/pallas_call | solution.py:457
  64.7 2.8 %add_convert_fusion = bf16[128,4096]{1,0:T(8,128)(2,1)} fusion(bf16[128,4096]{1,0:T(8,128)(2,1)} %get-tuple-element.8, bf16[128,4096]{1,0:T(8,128)(2,1)} %get-tuple-element.7), kind=kLoop, calls=%fused_computation | loop fusion | flops 2097152 | bytes 3145728 | tf_op jit(solution)/shard_map/convert_element_type | solution.py:519
